TPU v7x, 256 devices: a whole 4x4x8 slice. The times are simulated.
256 devices in a mesh: lib: 32 (over z, x_lo, core), ref: 8 (over y, x_hi).
Axes of the slice: x: 4 (x_hi: 2, x_lo: 2; x = x_hi * 2 + x_lo), y: 4, z: 8, core: 2. Of those that a mesh axis runs over, the one named last changes fastest.
Arguments:
- compounds: bfloat16 [262144, 512], P(('lib', 'ref')), may hold values from 0 to 2.5, as said below
- compound_weight: float32 [262144], P(('lib', 'ref')), may hold values from 0.5 to 12, as said below
- reference_prints: bfloat16 [4096, 512], P('ref'), may hold values from 0 to 2.5, as said below
- potency: bfloat16 [4096], P('ref'), may hold values from 4 to 10
- target_label: int32 [4096], P('ref'), may hold values from 0 to 255, as said below
Outputs:
- whitened: float32 [262144, 256], P(('lib', 'ref'))
Inputs may be any that keep to these rules, and one draw needn't show every extreme that they name: `target_label`: each of the 256 targets labels exactly 16 actives. `compounds`: nonnegative; every row has an entry of 0.25 or more. `reference_prints`: nonnegative; every row has an entry of 0.25 or more. `compound_weight`: positive.
All inputs are finite; a program needn't handle non-finite values.
Results may differ from a plain program's by a relative error of at most 0.0015.
Values may be sent and summed in bfloat16 or wider, within the bound.
No kernel may reach another device: no remote copies, remote signals or barrier semaphores. Data moves between devices by JAX's collectives and lax.ppermute only.
A program may use at most 64 MiB of HBM per device.

v0:
```python
import math

import jax
import jax.numpy as jnp
from jax import lax
from jax.sharding import PartitionSpec as P

TARGETS = 256


SHARPNESS = 320.0
SHRINKAGE = 0.02


def on_device(compounds, compound_weight, reference_prints, potency, target_label):
    query_count = compounds.shape[0]
    query_norm = jnp.sum(compounds.astype(jnp.float32) ** 2, axis=1)
    columns = jnp.arange(TARGETS, dtype=jnp.int32)
    start_state = (
        jnp.full((query_count,), -1e30, jnp.float32),
        jnp.zeros((query_count,), jnp.float32),
        jnp.zeros((query_count, TARGETS), jnp.float32),
    )
    every_print, every_potency, every_label = (
        lax.all_gather(reference_prints, "ref", axis=0, tiled=True),
        lax.all_gather(potency, "ref", axis=0, tiled=True),
        lax.all_gather(target_label, "ref", axis=0, tiled=True),
    )
    piece_rows = every_print.shape[0]
    block_rows = math.gcd(piece_rows, 512)

    def one_block(position, state):
        row_top, denominator, numerator = state
        slab = lax.dynamic_slice_in_dim(every_print, position * block_rows, block_rows, 0)
        slab_power = lax.dynamic_slice_in_dim(every_potency, position * block_rows, block_rows, 0)
        slab_target = lax.dynamic_slice_in_dim(every_label, position * block_rows, block_rows, 0)
        slab_norm = jnp.sum(slab.astype(jnp.float32) ** 2, axis=1)
        intersection = lax.dot_general(
            compounds, slab, (((1,), (1,)), ((), ())), preferred_element_type=jnp.float32
        )
        scores = (
            SHARPNESS * intersection / (query_norm[:, None] + slab_norm[None, :] - intersection)
        )
        new_top = jnp.maximum(row_top, jnp.max(scores, axis=1))
        expo = jnp.exp(scores - new_top[:, None]).astype(jnp.bfloat16)
        rescale = jnp.exp(row_top - new_top)
        values = (slab_target[:, None] == columns[None, :]).astype(jnp.bfloat16) * slab_power[
            :, None
        ]
        denominator = denominator * rescale + jnp.sum(expo.astype(jnp.float32), axis=1)
        numerator = numerator * rescale[:, None] + jnp.dot(
            expo, values, preferred_element_type=jnp.float32
        )
        return (new_top, denominator, numerator)

    row_top, denominator, numerator = lax.fori_loop(
        0, piece_rows // block_rows, one_block, start_state
    )
    profile = numerator / denominator[:, None]
    weighted = compound_weight[:, None] * profile
    identity = jnp.eye(TARGETS, dtype=jnp.float32)
    first_moment, weight_total = lax.psum(
        (jnp.sum(weighted, axis=0), jnp.sum(compound_weight)), ("lib", "ref")
    )
    average = first_moment / weight_total
    centered = profile - average[None, :]
    local_spread = jnp.dot(
        centered.T, compound_weight[:, None] * centered, precision=lax.Precision.HIGHEST
    )
    total_spread = lax.psum(local_spread, ("lib", "ref"))
    covariance = total_spread / weight_total + SHRINKAGE * identity
    factor = lax.linalg.cholesky(covariance)
    solved = lax.linalg.triangular_solve(factor, centered.T, left_side=True, lower=True)
    return solved.T * jnp.sqrt(compound_weight)[:, None]


def solution(mesh):
    placed = (P(("lib", "ref"), None), P(("lib", "ref")), P("ref", None), P("ref"), P("ref"))
    return jax.shard_map(
        on_device, mesh=mesh, in_specs=placed, out_specs=P(("lib", "ref"), None), check_vma=False
    )
```

profile of v0, /device:TPU:1, one launch (start us, length us, event | category | flops | bytes accessed | tf_op | source)
XLA Modules:
  0.0 527.0 jit_solution(4366402205074688304)
XLA Ops:
  8.0 26.3 %all-gather.1 = bf16[8,1,512]{2,1,0:T(2,128)(2,1)S(1)} all-gather(bf16[1,1,512]{2,1,0:T(2,128)(2,1)S(1)} %reshape.47), channel_id=1, replica_groups=mesh['lib'=32,'ref'=8] {'ref'}, dimensions={0}, use_global_device_ids=true | all-gather | bytes 9216 | tf_op jit(solution)/shard_map/all_gather | solution.py:26
  34.3 25.6 %all-gather = s32[8,1,512]{2,1,0:T(1,128)S(1)} all-gather(s32[1,1,512]{2,1,0:T(1,128)} %bitcast.50), channel_id=1, replica_groups=mesh['lib'=32,'ref'=8] {'ref'}, dimensions={0}, use_global_device_ids=true | all-gather | bytes 18432 | tf_op jit(solution)/shard_map/all_gather | solution.py:27
  59.9 1.5 multiply_reduce_fusion.1
  61.4 1.3 fusion.28
  62.8 27.2 %all-gather.4.cloned.1.call-done = bf16[4096,512]{1,0:T(8,128)(2,1)} async-done(((bf16[512,512]{1,0:T(8,128)(2,1)}), bf16[4096,512]{1,0:T(8,128)(2,1)}) %all-gather.4.cloned.1.call-update) | async-done | bytes 4194320 | tf_op jit(solution)/shard_map/all_gather | solution.py:25
  90.0 38.9 %while.20 = (s32[]{:T(128)}, f32[1024]{0:T(1024)S(1)}, f32[1024]{0:T(1024)S(1)}, f32[1024,256]{1,0:T(8,128)S(1)}, bf16[4096,512]{1,0:T(8,128)(2,1)}, /*index=5*/...) while((s32[]{:T(128)}, f32[1024]{0:T(1024)S(1)}, ...), condition=%wide.region_5.0_spmd.clone, body=%wide.region_1.0_spmd.clone.sunk | while | flops 812913152 | bytes 10568903 | solution.py:56
  91.2 2.2 fusion.42
  94.9 1.2 multiply_reduce_fusion.4
  96.1 2.2 fusion.42
  99.7 1.2 multiply_reduce_fusion.4
  100.9 2.2 fusion.42
  104.6 1.2 multiply_reduce_fusion.4
  105.8 2.2 fusion.42
  109.4 1.2 multiply_reduce_fusion.4
  110.7 2.2 fusion.42
  114.3 1.2 multiply_reduce_fusion.4
  115.5 2.2 fusion.42
  120.4 2.2 fusion.42
  125.2 2.2 fusion.42
  129.7 74.7 %all-reduce.1 = (f32[256]{0:T(256)S(1)}, f32[]{:T(128)}) all-reduce(f32[256]{0:T(256)S(1)} %multiply_reduce_fusion.2, f32[]{:T(128)} %get-tuple-element.266), channel_id=1, replica_groups=mesh['lib'=32,'ref'=8] {'lib','ref'}, use_global_device_ids=true, to_apply=%region_7.0 | all-reduce | flops 257 | bytes 2056 | tf_op jit(solution)/shard_map/psum | solution.py:62
  205.0 1.9 fusion.12
  207.2 245.7 %all-reduce.4.cloned.1.call-done = f32[256,256]{0,1:T(8,128)} async-done(((f32[256,256]{0,1:T(8,128)}), f32[256,256]{0,1:T(8,128)}) %all-reduce.4.cloned.1.call-update) | async-done | bytes 262160 | tf_op jit(solution)/shard_map/psum | solution.py:70
  452.9 1.6 select_add_fusion
  454.6 1.6 fusion.20
  456.3 11.7 %cholesky.49 = f32[128,128]{1,0:T(8,128)S(1)} custom-call(f32[128,128]{1,0:T(8,128)S(1)} %cholesky.115), custom_call_target="Cholesky" | custom-call | tf_op jit(solution)/shard_map/cholesky | solution.py:72
  468.0 9.8 %custom-call.11 = f32[1,128,128]{1,2,0:T(8,128)S(1)} custom-call(f32[1,128,128]{2,1,0:T(8,128)S(1)} %get-tuple-element.264), custom_call_target="InvertDiagBlocksLowerTriangular" | custom-call | tf_op jit(solution)/shard_map/cholesky | solution.py:72
  478.3 11.7 %cholesky.103 = f32[128,128]{1,0:T(8,128)S(1)} custom-call(f32[128,128]{1,0:T(8,128)S(1)} %convolution_subtract_fusion.1), custom_call_target="Cholesky" | custom-call | tf_op jit(solution)/shard_map/cholesky | solution.py:72
  492.6 4.3 while.19
  493.2 1.4 dynamic-slice.7
  495.4 1.4 dynamic-slice.7
  496.9 19.9 %custom-call.12 = f32[2,128,128]{1,2,0:T(8,128)S(1)} custom-call(f32[2,128,128]{2,1,0:T(8,128)S(1)} %get-tuple-element.184), custom_call_target="InvertDiagBlocksLowerTriangular" | custom-call | tf_op jit(solution)/shard_map/triangular_solve | solution.py:73
  518.9 1.3 copy.27
  (104 shorter events, 23.0 us)
Async XLA Ops:
  6.5 83.5 %all-gather.4.cloned.1.call-start = ((), (), s32[]{:S(2)}) async-start(), calls=%async_computation | async-start | bytes 4718592 | tf_op jit(solution)/shard_map/all_gather | solution.py:25
  7.3 445.6 %all-reduce.4.cloned.1.call-start = ((), (), s32[]{:S(2)}) async-start(), calls=%async_computation.1 | async-start | bytes 524288 | tf_op jit(solution)/shard_map/psum | solution.py:70
  128.9 0.7 copy-start
Sparse Core Ops, SparseCore 0:
  10.0 79.9 all-gather.3
  207.1 245.7 all-reduce.3
where the time goes:
time: 529 us; the launch traced here: 527 us
  waiting for transfers between devices  274 us (52%)
  blocking collectives  127 us (24%)
  other arithmetic  73.7 us (14%)
  matrix products  28.9 us (5%)
  between operations  15 us (3%)
  local copies, waits for them, and re-layouts  8.73 us (2%)
    psum x1, waiting for transfers between devices, on_device(): total_spread = lax.psum(local_spread, ('lib', 'ref'))  246 us
    psum x1, blocking collectives, on_device(): lax.psum((jnp.sum(weighted, axis=0), jnp.sum(compound_weight)), ('lib', '...  74.7 us
    another operation x6, other arithmetic, on_device(): factor = lax.linalg.cholesky(covariance)  34 us
    all_gather x1, waiting for transfers between devices, on_device(): lax.all_gather(reference_prints, 'ref', axis=0, tiled=True)  27.2 us
    all_gather x1, blocking collectives, on_device(): lax.all_gather(potency, 'ref', axis=0, tiled=True)  26.3 us
    all_gather x1, blocking collectives, on_device(): lax.all_gather(target_label, 'ref', axis=0, tiled=True)  25.6 us
    another operation x3, other arithmetic, on_device(): lax.linalg.triangular_solve(factor, centered.T, left_side=True, lower=True)  19.9 us
    dot_general x8, matrix products, one_block(): lax.dot_general(compounds, slab, (((1,), (1,)), ((), ())), preferred_elem...  17.7 us
  transfers between devices with their start and end apart: 2, of which 2 were waited for; matrix products, arithmetic and copies ran while one was open for 1% of the time, Pallas kernels for 0%

commit v1 on v0

v1 whole, which is shorter than its diff:
```python
import functools

import jax
import jax.numpy as jnp
from jax import lax
from jax.experimental import pallas as pl
from jax.experimental.pallas import tpu as pltpu
from jax.sharding import PartitionSpec as P

ALL = ("lib", "ref")
BITS = 512
EXTRA = 16
DEPTH = BITS + EXTRA
TARGETS = 256
SHRINKAGE = 0.02
LOG2E = 1.4426950408889634
SCALE = 320.0 * LOG2E
MARGIN = 58.0
BLOCK = 256
PANEL = 32
F32 = jnp.float32
BF16 = jnp.bfloat16
EXACT = lax.Precision.HIGHEST
VMEM = pl.BlockSpec(memory_space=pltpu.VMEM)


def params(mib=40):
    return pltpu.CompilerParams(vmem_limit_bytes=mib * 2**20)


def cost(flops, size):
    return pl.CostEstimate(flops=flops, bytes_accessed=size, transcendentals=0)


def place(x, y, z, c):
    return ((z % 8 * 2 + x % 2) * 2 + c % 2) * 8 + y % 4 * 2 + x // 2


def route(move):
    pairs = []
    for x in range(4):
        for y in range(4):
            for z in range(8):
                for c in range(2):
                    pairs.append((place(x, y, z, c), place(*move(x, y, z, c))))
    return sorted(pairs)


def send(value, move):
    return lax.ppermute(value, ALL, route(move))


def up(x, y, z, c):
    return x, y + 1, z, c


def down(x, y, z, c):
    return x, y - 1, z, c


def flip(x, y, z, c):
    return 3 - x, y, z, c


def sibling(x, y, z, c):
    return x, y, z, 1 - c


def prep_kernel(core_ref, prints_ref, potency_ref, label_ref, whole_ref, half_ref):
    prints = prints_ref[...].T
    wide = prints.astype(F32)
    norm = jnp.sum(wide * wide, axis=0, keepdims=True)
    high = norm.astype(BF16)
    rest = norm - high.astype(F32)
    middle = rest.astype(BF16)
    low = (rest - middle.astype(F32)).astype(BF16)
    row = lax.broadcasted_iota(jnp.int32, (EXTRA, prints.shape[1]), 0)
    extra = jnp.where(row == 0, potency_ref[...].astype(F32), 0.0)
    extra = jnp.where(row == 1, label_ref[...].astype(F32), extra)
    for at, part in ((2, high), (3, middle), (4, low)):
        extra = jnp.where(row == at, part.astype(F32), extra)
    extra = extra.astype(BF16)
    whole_ref[:BITS, :] = prints
    whole_ref[BITS:, :] = extra
    first = core_ref[0] == 0
    half = prints.shape[1] // 2

    @pl.when(first)
    def _():
        half_ref[:BITS, :] = prints[:, :half]
        half_ref[BITS:, :] = extra[:, :half]

    @pl.when(jnp.logical_not(first))
    def _():
        half_ref[:BITS, :] = prints[:, half:]
        half_ref[BITS:, :] = extra[:, half:]


def prepare(core, prints, potency, label):
    refs = prints.shape[0]
    return pl.pallas_call(
        prep_kernel,
        in_specs=[pl.BlockSpec(memory_space=pltpu.SMEM), VMEM, VMEM, VMEM],
        out_specs=[VMEM, VMEM],
        out_shape=[
            jax.ShapeDtypeStruct((DEPTH, refs), BF16),
            jax.ShapeDtypeStruct((DEPTH, refs // 2), BF16),
        ],
        compiler_params=params(),
        name="prepare",
    )(core, prints, potency, label)


def piece_scores(queries, query_norm, piece_ref):
    extra = piece_ref[BITS:, :].astype(F32)
    norm = extra[2:3] + extra[3:4] + extra[4:5]
    inter = jnp.dot(queries, piece_ref[:BITS, :], preferred_element_type=F32)
    inverse = 1.0 / ((query_norm + norm) - inter)
    return (inter * inverse) * SCALE


def piece_values(piece_ref):
    extra = piece_ref[BITS:, :].astype(F32)
    target = lax.broadcasted_iota(jnp.int32, (TARGETS, extra.shape[1]), 0)
    hit = target == extra[1:2].astype(jnp.int32)
    return jnp.where(hit, extra[0:1], 0.0).astype(BF16)


def add_piece(scores, top, piece_ref, num, den):
    expo = jnp.exp2(scores - top).astype(BF16)
    rounded = expo.astype(F32)
    for k in range(expo.shape[1] // 128):
        den = den + rounded[:, k * 128 : (k + 1) * 128]
    num = num + lax.dot_general(
        expo,
        piece_values(piece_ref),
        (((1,), (1,)), ((), ())),
        preferred_element_type=F32,
    )
    return num, den


def squared_norm(queries):
    wide = queries.astype(F32)
    return jnp.sum(wide * wide, axis=1, keepdims=True)


def first_kernel(queries_ref, piece_ref, num_ref, den_ref, top_ref):
    queries = queries_ref[...]
    rows = queries.shape[0]
    scores = piece_scores(queries, squared_norm(queries), piece_ref)
    top = jnp.max(scores, axis=1, keepdims=True) + MARGIN
    num = jnp.zeros((rows, TARGETS), F32)
    den = jnp.zeros((rows, 128), F32)
    num, den = add_piece(scores, top, piece_ref, num, den)
    num_ref[...] = num
    den_ref[...] = den
    top_ref[...] = jnp.broadcast_to(top, (rows, 128))


def more_kernel(count, *refs):
    queries_ref, num_in, den_in, top_ref = refs[:4]
    pieces = refs[4 : 4 + count]
    num_ref, den_ref = refs[4 + count :]
    queries = queries_ref[...]
    query_norm = squared_norm(queries)
    top = top_ref[:, 0:1]
    num, den = num_in[...], den_in[...]
    for piece_ref in pieces:
        scores = piece_scores(queries, query_norm, piece_ref)
        num, den = add_piece(scores, top, piece_ref, num, den)
    num_ref[...] = num
    den_ref[...] = den


def last_kernel(count, past, *refs):
    queries_ref, num_in, den_in, top_ref, weight_ref = refs[:5]
    pieces = refs[5 : 5 + count]
    earlier = refs[5 + count : 5 + count + past]
    profile_ref, moments_ref = refs[5 + count + past : 7 + count + past]
    buffers = refs[7 + count + past : -1]
    done = refs[-1]
    step = pl.program_id(0)
    rows = queries_ref.shape[0]
    queries = queries_ref[...]
    query_norm = squared_norm(queries)
    top = top_ref[:, 0:1]
    num, den = num_in[...], den_in[...]
    for piece_ref in pieces:
        scores = piece_scores(queries, query_norm, piece_ref)
        num, den = add_piece(scores, top, piece_ref, num, den)
    total = jnp.sum(den, axis=1, keepdims=True)
    here = pl.ds(pl.multiple_of(step * rows, rows), rows)
    profile_ref[here, :] = num * (1.0 / total)

    @pl.when(jnp.logical_not(jnp.max(total) <= 1.0))
    def _():
        copies = [
            pltpu.make_async_copy(source, buffer, done.at[k])
            for k, (source, buffer) in enumerate(zip(earlier, buffers))
        ]
        for copy in copies:
            copy.start()
        for copy in copies:
            copy.wait()
        everything = list(pieces) + list(buffers)
        best = jnp.full((rows, 1), -1.0, F32)
        for piece_ref in everything:
            scores = piece_scores(queries, query_norm, piece_ref)
            best = jnp.maximum(best, jnp.max(scores, axis=1, keepdims=True))
        again = jnp.zeros((rows, TARGETS), F32)
        weight = jnp.zeros((rows, 128), F32)
        for piece_ref in everything:
            scores = piece_scores(queries, query_norm, piece_ref)
            again, weight = add_piece(scores, best, piece_ref, again, weight)
        profile_ref[here, :] = again * (1.0 / jnp.sum(weight, axis=1, keepdims=True))

    @pl.when(step == pl.num_programs(0) - 1)
    def _():
        profile = profile_ref[...]
        weight = weight_ref[...]
        weight_total = jnp.sum(weight, axis=0, keepdims=True)
        first = jnp.sum(profile * weight, axis=0, keepdims=True)
        mean = first / weight_total
        spread = (profile - mean) * jnp.sqrt(weight)
        outer = (((0,), (0,)), ((), ()))
        moments = lax.dot_general(
            spread, spread, outer, precision=EXACT, preferred_element_type=F32
        ) + lax.dot_general(mean, first, outer, precision=EXACT, preferred_element_type=F32)
        row = lax.broadcasted_iota(jnp.int32, (TARGETS, TARGETS), 0)
        column = lax.broadcasted_iota(jnp.int32, (TARGETS, TARGETS), 1)
        moments = jnp.where((row == 0) & (column > 0), first, moments)
        moments = jnp.where((row == 1) & (column == 2), first[0:1, 0:1], moments)
        moments = jnp.where((row == 1) & (column == 3), weight_total, moments)
        moments_ref[...] = moments


def state_specs():
    return [
        pl.BlockSpec((BLOCK, BITS), lambda i: (i, 0)),
        pl.BlockSpec((BLOCK, TARGETS), lambda i: (i, 0)),
        pl.BlockSpec((BLOCK, 128), lambda i: (i, 0)),
        pl.BlockSpec((BLOCK, 128), lambda i: (i, 0)),
    ]


def whole(array):
    zeros = (0,) * array.ndim
    return pl.BlockSpec(array.shape, lambda i: zeros)


def work(rows, pieces):
    refs = sum(piece.shape[1] for piece in pieces)
    return cost(6 * rows * refs * (BITS + TARGETS), rows * 2048 + refs * DEPTH * 2)


def first_part(queries, piece):
    rows = queries.shape[0]
    specs = state_specs()
    return pl.pallas_call(
        first_kernel,
        grid=(rows // BLOCK,),
        in_specs=[specs[0], whole(piece)],
        out_specs=specs[1:],
        out_shape=[
            jax.ShapeDtypeStruct((rows, TARGETS), F32),
            jax.ShapeDtypeStruct((rows, 128), F32),
            jax.ShapeDtypeStruct((rows, 128), F32),
        ],
        compiler_params=params(),
        cost_estimate=work(rows, [piece]),
        name="first_part",
    )(queries, piece)


def more_part(queries, state, pieces):
    rows = queries.shape[0]
    specs = state_specs()
    num, den = pl.pallas_call(
        functools.partial(more_kernel, len(pieces)),
        grid=(rows // BLOCK,),
        in_specs=specs + [whole(piece) for piece in pieces],
        out_specs=specs[1:3],
        out_shape=[
            jax.ShapeDtypeStruct((rows, TARGETS), F32),
            jax.ShapeDtypeStruct((rows, 128), F32),
        ],
        compiler_params=params(),
        cost_estimate=work(rows, pieces),
        name="more_part",
    )(queries, *state, *pieces)
    return num, den, state[2]


def last_part(queries, state, weight, pieces, earlier):
    rows = queries.shape[0]
    return pl.pallas_call(
        functools.partial(last_kernel, len(pieces), len(earlier)),
        grid=(rows // BLOCK,),
        in_specs=state_specs()
        + [whole(weight)]
        + [whole(piece) for piece in pieces]
        + [pl.BlockSpec(memory_space=pl.ANY)] * len(earlier),
        out_specs=[
            pl.BlockSpec((rows, TARGETS), lambda i: (0, 0)),
            pl.BlockSpec((TARGETS, TARGETS), lambda i: (0, 0)),
        ],
        out_shape=[
            jax.ShapeDtypeStruct((rows, TARGETS), F32),
            jax.ShapeDtypeStruct((TARGETS, TARGETS), F32),
        ],
        scratch_shapes=[pltpu.VMEM(piece.shape, BF16) for piece in earlier]
        + [pltpu.SemaphoreType.DMA((len(earlier),))],
        compiler_params=params(),
        cost_estimate=work(rows, pieces),
        name="last_part",
    )(queries, *state, weight, *pieces, *earlier)


def repeat_row(block, at):
    return jnp.broadcast_to(block[at : at + 1, :], block.shape)


def inverse_factor(schur, size):
    groups = PANEL // 8
    panels = size // PANEL
    sub = lax.broadcasted_iota(jnp.int32, (8, 128), 0)
    eye = (
        lax.broadcasted_iota(jnp.int32, (PANEL, PANEL), 0)
        == lax.broadcasted_iota(jnp.int32, (PANEL, PANEL), 1)
    ).astype(F32)
    schur = [schur[i * PANEL : (i + 1) * PANEL, :] for i in range(panels)]
    inverse = [None] * panels
    result = []
    for t in range(panels):
        start = t * PANEL
        lane0 = start // 128 * 128
        left = schur[t][:, lane0:]
        right = [inverse[t]] if t else []
        right.append(eye)
        width = start + PANEL
        if width % 128:
            right.append(jnp.zeros((PANEL, -width % 128), F32))
        right = jnp.concatenate(right, axis=1)
        nl, nr = left.shape[1] // 128, right.shape[1] // 128
        tiles = [
            [left[8 * g : 8 * g + 8, 128 * k : 128 * k + 128] for k in range(nl)]
            + [right[8 * g : 8 * g + 8, 128 * k : 128 * k + 128] for k in range(nr)]
            for g in range(groups)
        ]
        square = left[:, start - lane0 : start - lane0 + PANEL]
        spread = [
            [
                jnp.broadcast_to(square[8 * g : 8 * g + 8, k : k + 1], (8, 128))
                if g >= k // 8
                else None
                for g in range(groups)
            ]
            for k in range(PANEL)
        ]
        inverses = []
        for k in range(PANEL):
            own, at = divmod(k, 8)
            inv = 1.0 / repeat_row(spread[k][own], at)
            inverses.append(inv)
            column = [
                spread[k][g] if g > own else jnp.where(sub > at, spread[k][g], 0.0) if g == own else None
                for g in range(groups)
            ]
            for m in range(k + 1, PANEL):
                factor = repeat_row(spread[k][m // 8], m % 8)
                for g in range(m // 8, groups):
                    spread[m][g] = spread[m][g] - (column[g] * factor) * inv
            multiple = [None if c is None else c * inv for c in column]
            for k2 in range(nl + nr):
                row = repeat_row(tiles[own][k2], at)
                for g in range(own, groups):
                    tiles[g][k2] = tiles[g][k2] - multiple[g] * row
        scale = []
        for g in range(groups):
            column = inverses[8 * g]
            for o in range(1, 8):
                column = jnp.where(sub == o, inverses[8 * g + o], column)
            scale.append(column)
        root = [jnp.sqrt(column) for column in scale]
        blank = [jnp.zeros((8, 128), F32)] * (size // 128 - nr)
        result.append(
            jnp.concatenate(
                [
                    jnp.concatenate([tiles[g][nl + k] * root[g] for k in range(nr)] + blank, axis=1)
                    for g in range(groups)
                ],
                axis=0,
            )
        )
        if t == panels - 1:
            break
        upper = jnp.concatenate([jnp.concatenate(tiles[g], axis=1) for g in range(groups)], axis=0)
        scaled = jnp.concatenate(
            [
                jnp.concatenate([tiles[g][k] * scale[g] for k in range(nl)], axis=1)
                for g in range(groups)
            ],
            axis=0,
        )
        for low, high in ((t + 1, t + 2), (t + 2, panels)):
            if low >= high:
                continue
            update = lax.dot_general(
                scaled[:, low * PANEL - lane0 : high * PANEL - lane0],
                upper,
                (((0,), (0,)), ((), ())),
                precision=EXACT,
                preferred_element_type=F32,
            )
            for i in range(low, high):
                part = update[(i - low) * PANEL : (i - low + 1) * PANEL]
                kept = [schur[i][:, :lane0]] if lane0 else []
                schur[i] = jnp.concatenate(kept + [schur[i][:, lane0:] - part[:, : nl * 128]], axis=1)
                fresh = -part[:, nl * 128 : nl * 128 + width]
                if inverse[i] is not None:
                    fresh = jnp.concatenate([inverse[i] + fresh[:, :start], fresh[:, start:]], axis=1)
                inverse[i] = fresh
    return jnp.concatenate(result, axis=0)


def whiten_kernel(moments_ref, profile_ref, weight_ref, out_ref):
    total = moments_ref[...]
    row = lax.broadcasted_iota(jnp.int32, (TARGETS, TARGETS), 0)
    column = lax.broadcasted_iota(jnp.int32, (TARGETS, TARGETS), 1)
    share = 1.0 / total[1:2, 3:4]
    first = jnp.where(column[0:1] == 0, total[1:2, 2:3], total[0:1, :])
    mean = first * share
    outer = lax.dot_general(
        mean, mean, (((0,), (0,)), ((), ())), precision=EXACT, preferred_element_type=F32
    )
    lower = jnp.where(column <= row, total, 0.0)
    strict = jnp.where(column < row, total, 0.0)
    covariance = (lower + strict.T) * share - outer
    covariance = covariance + jnp.where(row == column, SHRINKAGE, 0.0)
    inverse = inverse_factor(covariance, TARGETS)
    centered = (profile_ref[...] - mean) * jnp.sqrt(weight_ref[...])
    out_ref[...] = lax.dot_general(
        centered, inverse, (((1,), (1,)), ((), ())), precision=EXACT, preferred_element_type=F32
    )


def whiten(moments, profile, weight):
    return pl.pallas_call(
        whiten_kernel,
        in_specs=[VMEM, VMEM, VMEM],
        out_specs=VMEM,
        out_shape=jax.ShapeDtypeStruct(profile.shape, F32),
        compiler_params=params(),
        name="whiten",
    )(moments, profile, weight)


def on_device(compounds, compound_weight, reference_prints, potency, target_label):
    devices = lax.axis_size(ALL)
    core = lax.rem(lax.axis_index("lib"), 2).astype(jnp.int32).reshape(1)
    weight = compound_weight[:, None]
    own, half = prepare(core, reference_prints, potency[None, :], target_label[None, :])
    middle = half.shape[1] // 2

    flipped, above, below = send(half, flip), send(half, up), send(half, down)
    far_a = send(above[:, :middle], up)
    far_b = send(below[:, middle:], down)
    flipped_above, flipped_below = send(flipped, up), send(flipped, down)
    flipped_far_a = send(flipped_above[:, :middle], up)
    flipped_far_b = send(flipped_below[:, middle:], down)

    near = [flipped, above, below]
    near += [send(piece, sibling) for piece in near]
    later = [far_a, far_b, flipped_above, flipped_below, flipped_far_a, flipped_far_b]
    later += [send(piece, sibling) for piece in later]

    state = first_part(compounds, own)
    state = more_part(compounds, state, near)
    profile, moments = last_part(compounds, state, weight, later, [own] + near)

    shares = lax.all_to_all(moments.reshape(devices, 2, TARGETS // 2), ALL, 0, 0)
    share = jnp.sum(shares, axis=0, keepdims=True)
    total = lax.all_to_all(jnp.broadcast_to(share, shares.shape), ALL, 0, 0)
    return whiten(total.reshape(TARGETS, TARGETS), profile, weight)


def solution(mesh):
    placed = (P(("lib", "ref"), None), P(("lib", "ref")), P("ref", None), P("ref"), P("ref"))
    return jax.shard_map(
        on_device, mesh=mesh, in_specs=placed, out_specs=P(("lib", "ref"), None), check_vma=False
    )
```

time: 529 us -> 137 us (0.26)
  waiting for transfers between devices: 274 us -> 5.97 us
  blocking collectives: 127 us -> 49.8 us
  other arithmetic: 73.7 us -> 0.28 us
  Pallas kernels: 0 us -> 55.6 us
  matrix products: 28.9 us -> 0 us
  starting transfers between devices: 0.04 us -> 21.3 us
  between operations: 15 us -> 0.18 us
    psum x1 -> x0, waiting for transfers between devices: 246 us -> none  [on_device(): total_spread = lax.psum(local_spread, ('lib', 'ref'))]
    psum x1 -> x0, blocking collectives: 74.7 us -> none  [on_device(): lax.psum((jnp.sum(weighted, axis=0), jnp.sum(compound_weight)), ('lib', '...]
    pallas_call x0 -> x5, Pallas kernels: none -> 55.6 us  [the longest x1 34.9 us: last_part(): pl.pallas_call(functools.partial(last_kernel, len(pieces), len(earlier)),...]
    another operation x9 -> x0, other arithmetic: 54 us -> none  [the longest x6 34 us: on_device(): factor = lax.linalg.cholesky(covariance)]
    all_gather x2 -> x0, blocking collectives: 51.8 us -> none  [the longest x1 26.3 us: on_device(): lax.all_gather(potency, 'ref', axis=0, tiled=True)]
    all_to_all x0 -> x2, blocking collectives: none -> 49.8 us  [the longest x1 29.1 us: on_device(): lax.all_to_all(moments.reshape(devices, 2, TARGETS // 2), ALL, 0, 0)]
    all_gather x1 -> x0, waiting for transfers between devices: 27.2 us -> none  [on_device(): lax.all_gather(reference_prints, 'ref', axis=0, tiled=True)]
    dot_general x17 -> x0, matrix products: 26.5 us -> none  [the longest x8 17.7 us: one_block(): lax.dot_general(compounds, slab, (((1,), (1,)), ((), ())), preferred_elem...]
  transfers between devices with their start and end apart: 2 -> 18, of which waited for: 2 -> 2; matrix products, arithmetic and copies ran while one was open for 1% -> 1% of each run, Pallas kernels for 0% -> 7%
where the time goes in v1:
time: 137 us
  Pallas kernels  55.6 us (41%)
  blocking collectives  49.8 us (36%)
  starting transfers between devices  21.3 us (16%)
  waiting for transfers between devices  5.97 us (4%)
  local copies, waits for them, and re-layouts  3.57 us (3%)
    pallas_call x1, Pallas kernels, last_part(): pl.pallas_call(functools.partial(last_kernel, len(pieces), len(earlier)),...  34.9 us
    all_to_all x1, blocking collectives, on_device(): lax.all_to_all(moments.reshape(devices, 2, TARGETS // 2), ALL, 0, 0)  29.1 us
    ppermute x18, starting transfers between devices, send(): return lax.ppermute(value, ALL, route(move))  21.3 us
    all_to_all x1, blocking collectives, on_device(): total = lax.all_to_all(jnp.broadcast_to(share, shares.shape), ALL, 0, 0)  20.6 us
    pallas_call x1, Pallas kernels, whiten(): pl.pallas_call(whiten_kernel, in_specs=[VMEM, VMEM, VMEM], out_specs=VMEM...  10.8 us
    pallas_call x1, Pallas kernels, more_part(): pl.pallas_call(functools.partial(more_kernel, len(pieces)), grid=(rows //...  6.79 us
    ppermute x18, waiting for transfers between devices, send(): return lax.ppermute(value, ALL, route(move))  5.97 us
    pallas_call x1, Pallas kernels, first_part(): pl.pallas_call(first_kernel, grid=(rows // BLOCK,), in_specs=[specs[0], w...  2.91 us
  transfers between devices with their start and end apart: 18, of which 2 were waited for; matrix products, arithmetic and copies ran while one was open for 1% of the time, Pallas kernels for 7%

profile of v1, /device:TPU:1, one launch (start us, length us, event | category | flops | bytes accessed | tf_op | source)
XLA Modules:
  0.0 136.7 jit_solution(782666558996978474)
XLA Ops:
  0.0 0.7 copy-done.7
  0.7 0.7 copy-done.1
  1.4 1.0 copy-done
  2.4 0.2 prepare.1
  2.6 3.4 %collective-permute-start = (bf16[528,256]{1,0:T(8,128)(2,1)S(1)}, bf16[528,256]{1,0:T(8,128)(2,1)}, u32[]{:S(2)}, u32[]{:S(2)}) collective-permute-start(bf16[528,256]{1,0:T(8,128)(2,1)S(1)} %get-tuple-element.18), channel_id=1, source_target_pairs={{0,17},{1,16},{2,19},{3,18},{4,21},{5,20},{6,23},{7,22},{8,25},{9,... | collective-permute-start | bytes 811016 | tf_op jit(solution)/shard_map/ppermute | solution.py:50
  6.0 1.3 collective-permute-start.1
  7.3 1.4 %collective-permute-start.2 = (bf16[528,256]{1,0:T(8,128)(2,1)S(1)}, bf16[528,256]{1,0:T(8,128)(2,1)S(1)}, u32[]{:S(2)}, u32[]{:S(2)}) collective-permute-start(bf16[528,256]{1,0:T(8,128)(2,1)S(1)} %get-tuple-element.18), channel_id=1, source_target_pairs={{0,6},{1,7},{2,0},{3,1},{4,2},{5,3},{6,4},{7,5},{8,14},{9,15},{10,... | collective-permute-start | bytes 811016 | tf_op jit(solution)/shard_map/ppermute | solution.py:50
  8.8 2.4 %collective-permute-done.refs_4_.refs_18_ = bf16[528,256]{1,0:T(8,128)(2,1)} collective-permute-done((bf16[528,256]{1,0:T(8,128)(2,1)S(1)}, bf16[528,256]{1,0:T(8,128)(2,1)}, u32[]{:S(2)}, u32[]{:S(2)}) %collective-permute-start) | collective-permute-done | bytes 270368 | tf_op jit(solution)/shard_map/ppermute | solution.py:50
  11.2 2.3 %collective-permute-start.8 = (bf16[528,256]{1,0:T(8,128)(2,1)}, bf16[528,256]{1,0:T(8,128)(2,1)S(1)}, u32[]{:S(2)}, u32[]{:S(2)}) collective-permute-start(bf16[528,256]{1,0:T(8,128)(2,1)} %collective-permute-done.refs_4_.refs_18_), channel_id=1, source_target_pairs={{0,2},{1,3},{2,4},{3,5},{4,6},{5,7},{6,0},{7,1},{8,10},{9,11},{10,... | collective-permute-start | bytes 811016 | tf_op jit(solution)/shard_map/ppermute | solution.py:50
  13.5 1.4 %collective-permute-start.9 = (bf16[528,256]{1,0:T(8,128)(2,1)}, bf16[528,256]{1,0:T(8,128)(2,1)S(1)}, u32[]{:S(2)}, u32[]{:S(2)}) collective-permute-start(bf16[528,256]{1,0:T(8,128)(2,1)} %collective-permute-done.refs_4_.refs_18_), channel_id=1, source_target_pairs={{0,6},{1,7},{2,0},{3,1},{4,2},{5,3},{6,4},{7,5},{8,14},{9,15},{10,... | collective-permute-start | bytes 811016 | tf_op jit(solution)/shard_map/ppermute | solution.py:50
  15.0 2.0 %collective-permute-start.3 = (bf16[528,256]{1,0:T(8,128)(2,1)}, bf16[528,256]{1,0:T(8,128)(2,1)}, u32[]{:S(2)}, u32[]{:S(2)}) collective-permute-start(bf16[528,256]{1,0:T(8,128)(2,1)} %collective-permute-done.refs_4_.refs_18_), channel_id=1, source_target_pairs={{0,8},{1,9},{2,10},{3,11},{4,12},{5,13},{6,14},{7,15},{8,0},{9,1},... | collective-permute-start | bytes 811016 | tf_op jit(solution)/shard_map/ppermute | solution.py:50
  17.0 0.2 collective-permute-start.6
  17.2 0.7 slice.17
  17.9 2.6 %collective-permute-start.7 = (bf16[528,128]{1,0:T(8,128)(2,1)}, bf16[528,128]{1,0:T(8,128)(2,1)}, u32[]{:S(2)}, u32[]{:S(2)}) collective-permute-start(bf16[528,128]{1,0:T(8,128)(2,1)} %slice.17), channel_id=1, source_target_pairs={{0,6},{1,7},{2,0},{3,1},{4,2},{5,3},{6,4},{7,5},{8,14},{9,15},{10,... | collective-permute-start | bytes 405512 | tf_op jit(solution)/shard_map/ppermute | solution.py:50
  20.4 3.5 %collective-permute-done.6.refs_5_ = bf16[528,128]{1,0:T(8,128)(2,1)S(1)} collective-permute-done((bf16[528,128]{1,0:T(8,128)(2,1)S(1)}, bf16[528,128]{1,0:T(8,128)(2,1)S(1)}, u32[]{:S(2)}, u32[]{:S(2)}) %collective-permute-start.6) | collective-permute-done | bytes 135200 | tf_op jit(solution)/shard_map/ppermute | solution.py:50
  24.0 1.5 %collective-permute-start.4 = (bf16[528,256]{1,0:T(8,128)(2,1)S(1)}, bf16[528,256]{1,0:T(8,128)(2,1)}, u32[]{:S(2)}, u32[]{:S(2)}) collective-permute-start(bf16[528,256]{1,0:T(8,128)(2,1)S(1)} %collective-permute-done.1.refs_5_.refs_19_), channel_id=1, source_target_pairs={{0,8},{1,9},{2,10},{3,11},{4,12},{5,13},{6,14},{7,15},{8,0},{9,1},... | collective-permute-start | bytes 811016 | tf_op jit(solution)/shard_map/ppermute | solution.py:50
  25.6 0.2 copy.6.refs_4_.weight_ref
  25.9 0.5 collective-permute-start.12
  26.5 2.7 %collective-permute-start.11 = (bf16[528,128]{1,0:T(8,128)(2,1)S(1)}, bf16[528,128]{1,0:T(8,128)(2,1)S(1)}, u32[]{:S(2)}, u32[]{:S(2)}) collective-permute-start(bf16[528,128]{1,0:T(8,128)(2,1)S(1)} %slice.19), channel_id=1, source_target_pairs={{0,6},{1,7},{2,0},{3,1},{4,2},{5,3},{6,4},{7,5},{8,14},{9,15},{10,... | collective-permute-start | bytes 405512 | tf_op jit(solution)/shard_map/ppermute | solution.py:50
  29.2 2.9 %first_part.1 = (f32[1024,256]{1,0:T(8,128)S(1)}, f32[1024,128]{1,0:T(8,128)S(1)}, f32[1024,128]{1,0:T(8,128)S(1)}) custom-call(bf16[1024,512]{1,0:T(8,128)(2,1)S(1)} %copy-done.2, bf16[528,512]{1,0:T(8,128)(2,1)S(1)} %get-tuple-element.14.piece_ref.refs_17_), custom_call_target="tpu_custom_call" | custom-call | flops 2415919104 | bytes 2637824 | tf_op jit(solution)/shard_map/first_part/pallas_call | solution.py:260
  32.1 0.7 collective-permute-start.13
  32.8 0.1 collective-permute-start.14
  32.9 0.4 collective-permute-start.15
  33.3 0.4 collective-permute-start.16
  33.7 0.2 collective-permute-start.17
  33.9 6.8 %more_part.1 = (f32[1024,256]{1,0:T(8,128)S(1)}, f32[1024,128]{1,0:T(8,128)S(1)}) custom-call(bf16[1024,512]{1,0:T(8,128)(2,1)S(1)} %copy-done.2, f32[1024,256]{1,0:T(8,128)S(1)} %get-tuple-element.15.refs_1_, f32[1024,128]{1,0:T(8,128)S(1)} %get-tuple-element.16.refs_2_, f32[1024,128]{1,0:T(8,128)S(1)} %get-tuple-element.17.refs_3_, ...), custom_call_target="tpu_custom_call" | custom-call | flops 7247757312 | bytes 3719168 | tf_op jit(solution)/shard_map/more_part/pallas_call | solution.py:279
  40.7 34.9 %last_part.1 = (f32[1024,256]{1,0:T(8,128)S(1)}, f32[256,256]{1,0:T(8,128)S(1)}) custom-call(bf16[1024,512]{1,0:T(8,128)(2,1)S(1)} %copy-done.3, f32[1024,256]{1,0:T(8,128)S(1)} %get-tuple-element.19.refs_1_, f32[1024,128]{1,0:T(8,128)S(1)} %get-tuple-element.20.refs_2_, f32[1024,128]{1,0:T(8,128)S(1)} %get-tuple-element.17.refs_3_, ...), custom_call_target="tpu_custom_call" | custom-call | flops 9663676416 | bytes 4259840 | tf_op jit(solution)/shard_map/last_part/pallas_call | solution.py:297
  75.6 0.1 reshape.11
  75.8 29.1 %all_to_all.10 = f32[256,2,128]{2,1,0:T(2,128)S(1)} all-to-all(f32[256,2,128]{2,1,0:T(2,128)S(1)} %reshape.11), channel_id=1, replica_groups=mesh['lib'=32,'ref'=8] {'lib','ref'}, dimensions={0} | all-to-all | bytes 524288 | tf_op jit(solution)/shard_map/all_to_all | solution.py:482
  104.9 0.3 reduce_sum.9
  105.3 20.6 %all_to_all.11 = f32[256,2,128]{2,1,0:T(2,128)S(1)} all-to-all(f32[256,2,128]{2,1,0:T(2,128)S(1)} %broadcast_in_dim.18), channel_id=1, replica_groups=mesh['lib'=32,'ref'=8] {'lib','ref'}, dimensions={0} | all-to-all | bytes 524288 | tf_op jit(solution)/shard_map/all_to_all | solution.py:484
  125.9 10.8 %whiten.1 = f32[1024,256]{1,0:T(8,128)} custom-call(f32[256,256]{1,0:T(8,128)S(1)} %bitcast.7, f32[1024,256]{1,0:T(8,128)S(1)} %get-tuple-element.22.profile_ref, f32[1024,1]{1,0:T(8,128)S(1)} %copy.6.refs_4_.weight_ref), custom_call_target="tpu_custom_call" | custom-call | tf_op jit(solution)/shard_map/whiten/pallas_call | solution.py:449
  (37 shorter events, 0.4 us)
Async XLA Ops:
  0.0 0.7 copy-start.7
  0.7 0.7 copy-start.1
  1.4 1.0 copy-start
  2.4 26.8 %copy-start.2 = (bf16[1024,512]{1,0:T(8,128)(2,1)S(1)}, bf16[1024,512]{1,0:T(8,128)(2,1)}, u32[]{:S(2)}) copy-start(bf16[1024,512]{1,0:T(8,128)(2,1)} %refs_0_.3) | copy-start | bytes 3145732
  2.6 8.5 %collective-permute-start = (bf16[528,256]{1,0:T(8,128)(2,1)S(1)}, bf16[528,256]{1,0:T(8,128)(2,1)}, u32[]{:S(2)}, u32[]{:S(2)}) collective-permute-start(bf16[528,256]{1,0:T(8,128)(2,1)S(1)} %get-tuple-element.18), channel_id=1, source_target_pairs={{0,17},{1,16},{2,19},{3,18},{4,21},{5,20},{6,23},{7,22},{8,25},{9,... | collective-permute-start | bytes 811016 | tf_op jit(solution)/shard_map/ppermute | solution.py:50
  6.0 10.9 %collective-permute-start.1 = (bf16[528,256]{1,0:T(8,128)(2,1)S(1)}, bf16[528,256]{1,0:T(8,128)(2,1)S(1)}, u32[]{:S(2)}, u32[]{:S(2)}) collective-permute-start(bf16[528,256]{1,0:T(8,128)(2,1)S(1)} %get-tuple-element.18), channel_id=1, source_target_pairs={{0,2},{1,3},{2,4},{3,5},{4,6},{5,7},{6,0},{7,1},{8,10},{9,11},{10,... | collective-permute-start | bytes 811016 | tf_op jit(solution)/shard_map/ppermute | solution.py:50
  7.3 9.9 %collective-permute-start.2 = (bf16[528,256]{1,0:T(8,128)(2,1)S(1)}, bf16[528,256]{1,0:T(8,128)(2,1)S(1)}, u32[]{:S(2)}, u32[]{:S(2)}) collective-permute-start(bf16[528,256]{1,0:T(8,128)(2,1)S(1)} %get-tuple-element.18), channel_id=1, source_target_pairs={{0,6},{1,7},{2,0},{3,1},{4,2},{5,3},{6,4},{7,5},{8,14},{9,15},{10,... | collective-permute-start | bytes 811016 | tf_op jit(solution)/shard_map/ppermute | solution.py:50
  11.2 14.3 %collective-permute-start.8 = (bf16[528,256]{1,0:T(8,128)(2,1)}, bf16[528,256]{1,0:T(8,128)(2,1)S(1)}, u32[]{:S(2)}, u32[]{:S(2)}) collective-permute-start(bf16[528,256]{1,0:T(8,128)(2,1)} %collective-permute-done.refs_4_.refs_18_), channel_id=1, source_target_pairs={{0,2},{1,3},{2,4},{3,5},{4,6},{5,7},{6,0},{7,1},{8,10},{9,11},{10,... | collective-permute-start | bytes 811016 | tf_op jit(solution)/shard_map/ppermute | solution.py:50
  13.5 12.3 %collective-permute-start.9 = (bf16[528,256]{1,0:T(8,128)(2,1)}, bf16[528,256]{1,0:T(8,128)(2,1)S(1)}, u32[]{:S(2)}, u32[]{:S(2)}) collective-permute-start(bf16[528,256]{1,0:T(8,128)(2,1)} %collective-permute-done.refs_4_.refs_18_), channel_id=1, source_target_pairs={{0,6},{1,7},{2,0},{3,1},{4,2},{5,3},{6,4},{7,5},{8,14},{9,15},{10,... | collective-permute-start | bytes 811016 | tf_op jit(solution)/shard_map/ppermute | solution.py:50
  15.0 11.5 %collective-permute-start.3 = (bf16[528,256]{1,0:T(8,128)(2,1)}, bf16[528,256]{1,0:T(8,128)(2,1)}, u32[]{:S(2)}, u32[]{:S(2)}) collective-permute-start(bf16[528,256]{1,0:T(8,128)(2,1)} %collective-permute-done.refs_4_.refs_18_), channel_id=1, source_target_pairs={{0,8},{1,9},{2,10},{3,11},{4,12},{5,13},{6,14},{7,15},{8,0},{9,1},... | collective-permute-start | bytes 811016 | tf_op jit(solution)/shard_map/ppermute | solution.py:50
  17.0 7.0 %collective-permute-start.6 = (bf16[528,128]{1,0:T(8,128)(2,1)S(1)}, bf16[528,128]{1,0:T(8,128)(2,1)S(1)}, u32[]{:S(2)}, u32[]{:S(2)}) collective-permute-start(bf16[528,128]{1,0:T(8,128)(2,1)S(1)} %slice.16), channel_id=1, source_target_pairs={{0,2},{1,3},{2,4},{3,5},{4,6},{5,7},{6,0},{7,1},{8,10},{9,11},{10,... | collective-permute-start | bytes 405512 | tf_op jit(solution)/shard_map/ppermute | solution.py:50
  17.2 8.4 %copy-start.6 = (f32[1024]{0:T(1024)S(1)}, f32[1024]{0:T(1024)}, u32[]{:S(2)}) copy-start(f32[1024]{0:T(1024)} %param.6) | copy-start | bytes 12292
  17.9 8.5 %collective-permute-start.7 = (bf16[528,128]{1,0:T(8,128)(2,1)}, bf16[528,128]{1,0:T(8,128)(2,1)}, u32[]{:S(2)}, u32[]{:S(2)}) collective-permute-start(bf16[528,128]{1,0:T(8,128)(2,1)} %slice.17), channel_id=1, source_target_pairs={{0,6},{1,7},{2,0},{3,1},{4,2},{5,3},{6,4},{7,5},{8,14},{9,15},{10,... | collective-permute-start | bytes 405512 | tf_op jit(solution)/shard_map/ppermute | solution.py:50
  24.0 1.9 %copy-start.4 = (bf16[528,128]{1,0:T(8,128)(2,1)}, bf16[528,128]{1,0:T(8,128)(2,1)S(1)}, u32[]{:S(2)}) copy-start(bf16[528,128]{1,0:T(8,128)(2,1)S(1)} %collective-permute-done.6.refs_5_) | copy-start | bytes 405508
  24.0 8.1 %collective-permute-start.4 = (bf16[528,256]{1,0:T(8,128)(2,1)S(1)}, bf16[528,256]{1,0:T(8,128)(2,1)}, u32[]{:S(2)}, u32[]{:S(2)}) collective-permute-start(bf16[528,256]{1,0:T(8,128)(2,1)S(1)} %collective-permute-done.1.refs_5_.refs_19_), channel_id=1, source_target_pairs={{0,8},{1,9},{2,10},{3,11},{4,12},{5,13},{6,14},{7,15},{8,0},{9,1},... | collective-permute-start | bytes 811016 | tf_op jit(solution)/shard_map/ppermute | solution.py:50
  25.5 7.3 %collective-permute-start.5 = (bf16[528,256]{1,0:T(8,128)(2,1)S(1)}, bf16[528,256]{1,0:T(8,128)(2,1)}, u32[]{:S(2)}, u32[]{:S(2)}) collective-permute-start(bf16[528,256]{1,0:T(8,128)(2,1)S(1)} %collective-permute-done.2.refs_6_.refs_20_), channel_id=1, source_target_pairs={{0,8},{1,9},{2,10},{3,11},{4,12},{5,13},{6,14},{7,15},{8,0},{9,1},... | collective-permute-start | bytes 811016 | tf_op jit(solution)/shard_map/ppermute | solution.py:50
  25.9 7.1 %collective-permute-start.12 = (bf16[528,128]{1,0:T(8,128)(2,1)S(1)}, bf16[528,128]{1,0:T(8,128)(2,1)S(1)}, u32[]{:S(2)}, u32[]{:S(2)}) collective-permute-start(bf16[528,128]{1,0:T(8,128)(2,1)S(1)} %collective-permute-done.6.refs_5_), channel_id=1, source_target_pairs={{0,8},{1,9},{2,10},{3,11},{4,12},{5,13},{6,14},{7,15},{8,0},{9,1},... | collective-permute-start | bytes 405512 | tf_op jit(solution)/shard_map/ppermute | solution.py:50
  26.4 6.9 %collective-permute-start.10 = (bf16[528,128]{1,0:T(8,128)(2,1)S(1)}, bf16[528,128]{1,0:T(8,128)(2,1)S(1)}, u32[]{:S(2)}, u32[]{:S(2)}) collective-permute-start(bf16[528,128]{1,0:T(8,128)(2,1)S(1)} %slice.18), channel_id=1, source_target_pairs={{0,2},{1,3},{2,4},{3,5},{4,6},{5,7},{6,0},{7,1},{8,10},{9,11},{10,... | collective-permute-start | bytes 405512 | tf_op jit(solution)/shard_map/ppermute | solution.py:50
  26.5 7.2 %collective-permute-start.11 = (bf16[528,128]{1,0:T(8,128)(2,1)S(1)}, bf16[528,128]{1,0:T(8,128)(2,1)S(1)}, u32[]{:S(2)}, u32[]{:S(2)}) collective-permute-start(bf16[528,128]{1,0:T(8,128)(2,1)S(1)} %slice.19), channel_id=1, source_target_pairs={{0,6},{1,7},{2,0},{3,1},{4,2},{5,3},{6,4},{7,5},{8,14},{9,15},{10,... | collective-permute-start | bytes 405512 | tf_op jit(solution)/shard_map/ppermute | solution.py:50
  32.1 8.6 %collective-permute-start.13 = (bf16[528,128]{1,0:T(8,128)(2,1)}, bf16[528,128]{1,0:T(8,128)(2,1)S(1)}, u32[]{:S(2)}, u32[]{:S(2)}) collective-permute-start(bf16[528,128]{1,0:T(8,128)(2,1)} %collective-permute-done.7.refs_6_), channel_id=1, source_target_pairs={{0,8},{1,9},{2,10},{3,11},{4,12},{5,13},{6,14},{7,15},{8,0},{9,1},... | collective-permute-start | bytes 405512 | tf_op jit(solution)/shard_map/ppermute | solution.py:50
  32.8 7.9 %collective-permute-start.14 = (bf16[528,256]{1,0:T(8,128)(2,1)S(1)}, bf16[528,256]{1,0:T(8,128)(2,1)S(1)}, u32[]{:S(2)}, u32[]{:S(2)}) collective-permute-start(bf16[528,256]{1,0:T(8,128)(2,1)S(1)} %collective-permute-done.8.refs_7_), channel_id=1, source_target_pairs={{0,8},{1,9},{2,10},{3,11},{4,12},{5,13},{6,14},{7,15},{8,0},{9,1},... | collective-permute-start | bytes 811016 | tf_op jit(solution)/shard_map/ppermute | solution.py:50
  32.9 7.8 %collective-permute-start.15 = (bf16[528,256]{1,0:T(8,128)(2,1)S(1)}, bf16[528,256]{1,0:T(8,128)(2,1)S(1)}, u32[]{:S(2)}, u32[]{:S(2)}) collective-permute-start(bf16[528,256]{1,0:T(8,128)(2,1)S(1)} %collective-permute-done.9.refs_8_), channel_id=1, source_target_pairs={{0,8},{1,9},{2,10},{3,11},{4,12},{5,13},{6,14},{7,15},{8,0},{9,1},... | collective-permute-start | bytes 811016 | tf_op jit(solution)/shard_map/ppermute | solution.py:50
  33.3 7.3 %collective-permute-start.16 = (bf16[528,128]{1,0:T(8,128)(2,1)S(1)}, bf16[528,128]{1,0:T(8,128)(2,1)S(1)}, u32[]{:S(2)}, u32[]{:S(2)}) collective-permute-start(bf16[528,128]{1,0:T(8,128)(2,1)S(1)} %collective-permute-done.10.refs_9_), channel_id=1, source_target_pairs={{0,8},{1,9},{2,10},{3,11},{4,12},{5,13},{6,14},{7,15},{8,0},{9,1},... | collective-permute-start | bytes 405512 | tf_op jit(solution)/shard_map/ppermute | solution.py:50
  33.7 7.0 %collective-permute-start.17 = (bf16[528,128]{1,0:T(8,128)(2,1)S(1)}, bf16[528,128]{1,0:T(8,128)(2,1)S(1)}, u32[]{:S(2)}, u32[]{:S(2)}) collective-permute-start(bf16[528,128]{1,0:T(8,128)(2,1)S(1)} %collective-permute-done.11.refs_10_), channel_id=1, source_target_pairs={{0,8},{1,9},{2,10},{3,11},{4,12},{5,13},{6,14},{7,15},{8,0},{9,1},... | collective-permute-start | bytes 405512 | tf_op jit(solution)/shard_map/ppermute | solution.py:50
  33.9 6.9 %copy-start.3 = (bf16[1024,512]{1,0:T(8,128)(2,1)S(1)}, bf16[1024,512]{1,0:T(8,128)(2,1)}, u32[]{:S(2)}) copy-start(bf16[1024,512]{1,0:T(8,128)(2,1)} %refs_0_.3) | copy-start | bytes 3145732
  33.9 6.9 %copy-start.5 = (bf16[528,128]{1,0:T(8,128)(2,1)S(1)}, bf16[528,128]{1,0:T(8,128)(2,1)}, u32[]{:S(2)}) copy-start(bf16[528,128]{1,0:T(8,128)(2,1)} %copy-done.4) | copy-start | bytes 405508
